TPU v7x, 32 devices: a whole 2x2x4 slice. The times are simulated.
32 devices in a mesh: members: 2 (over x), band: 16 (over z, y, core).
Axes of the slice: x: 2, y: 2, z: 4, core: 2. Of those that a mesh axis runs over, the one named last changes fastest.
Arguments:
- grid_inputs: bfloat16 [96, 384, 256], P(('members', 'band')), parts along dimension 0, may hold values from -6 to 6
- stencil_prenorm_scale: float32 [256], replicated, may hold values from 0.1 to 1.9
- patch_kernel_profiles: float32 [48, 9, 27], P('band'), may hold values from -1.2 to 1.2
- channel_mixer_tensor: bfloat16 [2304, 256], replicated, may hold values from -0.125 to 0.125
- softmax_prenorm_scale: float32 [256], replicated, may hold values from 0.1 to 1.9
- probe_lookup_content_projector: bfloat16 [256, 768], replicated, may hold values from -0.375 to 0.375
- head_logit_scales: float32 [8], replicated, may hold values from 3 to 500
- final_projector: bfloat16 [256, 256], replicated, may hold values from -0.375 to 0.375
- azimuth_reaches: int32 [48, 5], P('band'), may hold values from 1 to 8, as said below
Outputs:
- encoded: bfloat16 [96, 384, 256], P(('members', 'band')), parts along dimension 0
There are 2 independent parts, one for each index of `members`. A program takes and returns all parts, laid end to end along the dimension named above; an argument that names none is the same for every part. Nothing has to cross between parts.
Inputs may be any that keep to these rules, and one draw needn't show every extreme that they name: azimuth_reaches[i, a] is the longitude reach of row i's disc in its row at offset a - 2; the rows at the poles reach 8.
All inputs are finite; a program needn't handle non-finite values.
Results may differ from a plain program's by a relative error of at most 0.025.
The roundings to bfloat16 on the way count: a program that leaves them out, or rounds other values in their place, can miss the bound.
Values may be sent and summed in bfloat16 or wider, within the bound.
A program may use at most 64 MiB of HBM per device.

v0:
```python
import functools
import math

import jax
import jax.numpy as jnp
from jax import lax
from jax.experimental import pallas as pl
from jax.experimental.pallas import tpu as pltpu
from jax.sharding import PartitionSpec as P

HEAD_COUNT = 8
HEAD_WIDTH = 32
BASIS_COUNT = 9
CONV_REACH = 4
PATCH_LAT_EXTENT = 2
DISC_REACH = 8
EPSILON = 1e-06

TAPS = 2 * CONV_REACH + 1
CONV_BLOCK = 64
CONV_WINDOW = CONV_BLOCK + 16
QUERY_BLOCK = 32
KEY_WINDOW = QUERY_BLOCK + 2 * DISC_REACH
KEYS = 256
GROUP = 4
ROWS_A = 2 * PATCH_LAT_EXTENT + 1
PAD = DISC_REACH
TAIL = 24
LOG2E = math.log2(math.e)
F32 = jnp.float32
BF16 = jnp.bfloat16


def rms(values, gain):
    inverse = lax.rsqrt(jnp.mean(values * values, axis=-1, keepdims=True) + EPSILON)
    return values * inverse * gain


def ring_pad(row):
    return jnp.concatenate([row[-PAD:], row, row[:TAIL]], axis=0)


def half_turn(row):
    half = row.shape[0] // 2
    return jnp.concatenate([row[half:], row[:half]], axis=0)


def kernel(
    n,
    x_hbm,
    gain1_hbm,
    prof_hbm,
    mix_hbm,
    gain2_hbm,
    proj_hbm,
    scale_hbm,
    final_hbm,
    reach_hbm,
    out_ref,
    x_ref,
    gain1_ref,
    prof_ref,
    mix_ref,
    gain2_ref,
    proj_ref,
    scale_ref,
    final_ref,
    reach_ref,
    xhalo,
    ext,
    taps,
    toeplitz,
    basis,
    hidden,
    att,
    queries,
    keys,
    values,
    bias,
    heads,
    mixture,
    send_x,
    recv_x,
    send_a,
    recv_a,
    loads,
):
    rows, longitudes, channels = x_ref.shape
    me = lax.axis_index("band")
    has_up = me > 0
    has_down = me < n - 1
    depth = PATCH_LAT_EXTENT
    sent = longitudes + 16

    def x_copy(side):
        return pltpu.make_async_remote_copy(
            src_ref=x_hbm.at[0 if side == 0 else rows - 1],
            dst_ref=xhalo.at[1 - side],
            send_sem=send_x.at[side],
            recv_sem=recv_x.at[1 - side],
            device_id={"band": me - 1 if side == 0 else me + 1},
            device_id_type=pl.DeviceIdType.MESH,
        )

    def a_copy(side, step):
        source = depth + step if side == 0 else rows + step
        target = rows + depth + step if side == 0 else step
        slot = side * depth + step
        other = (1 - side) * depth + step
        return pltpu.make_async_remote_copy(
            src_ref=att.at[source, pl.ds(0, sent)],
            dst_ref=att.at[target, pl.ds(0, sent)],
            send_sem=send_a.at[slot],
            recv_sem=recv_a.at[other],
            device_id={"band": me - 1 if side == 0 else me + 1},
            device_id_type=pl.DeviceIdType.MESH,
        )

    has = (has_up, has_down)

    pairs = (
        (x_hbm, x_ref),
        (gain1_hbm, gain1_ref),
        (reach_hbm, reach_ref),
        (prof_hbm, prof_ref),
        (mix_hbm, mix_ref),
        (gain2_hbm, gain2_ref),
        (proj_hbm, proj_ref),
        (scale_hbm, scale_ref),
        (final_hbm, final_ref),
    )
    fetch = [
        pltpu.make_async_copy(source, target, loads.at[i])
        for i, (source, target) in enumerate(pairs)
    ]
    for copy in fetch:
        copy.start()

    barrier = pltpu.get_barrier_semaphore()
    for side in range(2):

        @pl.when(has[side])
        def _():
            pl.semaphore_signal(
                barrier,
                inc=1,
                device_id={"band": me - 1 if side == 0 else me + 1},
                device_id_type=pl.DeviceIdType.MESH,
            )

    pl.semaphore_wait(barrier, jnp.where(me == 0, 1, 2) - jnp.where(me == n - 1, 1, 0))

    for side in range(2):

        @pl.when(has[side])
        def _():
            x_copy(side).start()

    shape2 = (HEAD_COUNT * QUERY_BLOCK, channels)
    sub = lax.broadcasted_iota(jnp.int32, shape2, 0)
    lane = lax.broadcasted_iota(jnp.int32, shape2, 1)
    heads[...] = jnp.where(sub // QUERY_BLOCK == lane // HEAD_WIDTH, 1.0, 0.0).astype(BF16)
    ones_blocks = heads if QUERY_BLOCK == HEAD_WIDTH else None

    key = lax.broadcasted_iota(jnp.int32, (QUERY_BLOCK, KEYS), 1)
    query = lax.broadcasted_iota(jnp.int32, (QUERY_BLOCK, KEYS), 0)
    fetch[2].wait()
    for r in range(rows):
        limit = jnp.zeros((QUERY_BLOCK, KEYS), jnp.int32)
        start = jnp.zeros((QUERY_BLOCK, KEYS), jnp.int32)
        for a in range(ROWS_A):
            inside = key >= a * KEY_WINDOW
            limit = jnp.where(inside, reach_ref[r, a], limit)
            start = jnp.where(inside, a * KEY_WINDOW, start)
        distance = jnp.abs(key - start - DISC_REACH - query)
        bias[r] = jnp.where(distance <= limit, 0.0, -1e30).astype(F32)

    fetch[0].wait()
    fetch[1].wait()
    gain1 = gain1_ref[...]

    for r in range(rows):
        ext[r + 1] = ring_pad(rms(x_ref[r].astype(F32), gain1)).astype(BF16)

    tap_lane = lax.broadcasted_iota(jnp.int32, (16, KEYS), 1)

    def build_filters(r):
        taps[...] = jnp.zeros_like(taps)
        taps[0:BASIS_COUNT, 0 : 3 * TAPS] = prof_ref[:, r, :]
        flat = taps[...]
        placed = jnp.zeros_like(flat)
        for a in range(3):
            begin = a * CONV_WINDOW + CONV_REACH
            moved = pltpu.roll(flat, begin - a * TAPS, axis=1) if begin - a * TAPS else flat
            offset = tap_lane - begin
            reach = jnp.minimum(reach_ref[r, PATCH_LAT_EXTENT - 1 + a], CONV_REACH)
            inside = jnp.abs(offset - CONV_REACH) <= reach
            placed = jnp.where(inside, moved, placed)
        for k in range(BASIS_COUNT):
            spread = jnp.broadcast_to(placed[k : k + 1], (CONV_BLOCK, KEYS))
            spread = pltpu.roll(spread, 0, axis=1, stride=1, stride_axis=0)
            toeplitz[k * CONV_BLOCK : (k + 1) * CONV_BLOCK] = spread.astype(BF16)

    fetch[3].wait()

    def conv_row(r, first=False):
        build_filters(r)

        def conv_block(b, carry):
            at = pl.multiple_of(b * CONV_BLOCK, CONV_BLOCK)
            window = jnp.concatenate(
                [
                    ext[r, pl.ds(at, CONV_WINDOW)],
                    ext[r + 1, pl.ds(at, CONV_WINDOW)],
                    ext[r + 2, pl.ds(at, KEYS - 2 * CONV_WINDOW)],
                ],
                axis=0,
            )
            sums = jnp.dot(toeplitz[...], window, preferred_element_type=F32).astype(BF16)
            for k in range(BASIS_COUNT):
                basis[pl.ds(at, CONV_BLOCK), k * channels : (k + 1) * channels] = sums[
                    k * CONV_BLOCK : (k + 1) * CONV_BLOCK
                ]
            return carry

        lax.fori_loop(0, longitudes // CONV_BLOCK, conv_block, 0, unroll=2)
        if first:
            fetch[4].wait()
            fetch[5].wait()
            fetch[6].wait()
        gain2 = gain2_ref[...]
        mixed = jnp.dot(basis[...], mix_ref[...], preferred_element_type=F32)
        total = x_ref[r].astype(F32) + mixed
        hidden[r] = total
        normed = rms(total, gain2)
        att[r + depth] = ring_pad(normed).astype(BF16)
        queries[r] = unit(
            jnp.dot(
                normed.astype(BF16), proj_ref[:, 0:channels], preferred_element_type=F32
            )
        )

        if r < depth:

            @pl.when(has_up)
            def _():
                a_copy(0, r).start()

            if r == 0 or r == 1:

                @pl.when(jnp.logical_not(has_up))
                def _():
                    att[depth - 1 - r] = ring_pad(half_turn(normed)).astype(BF16)

        if r >= rows - depth:

            @pl.when(has_down)
            def _():
                a_copy(1, r - (rows - depth)).start()

            @pl.when(jnp.logical_not(has_down))
            def _():
                att[2 * rows + 2 * depth - 1 - (r + depth) + 0] = ring_pad(
                    half_turn(normed)
                ).astype(BF16)

    def unit(product):
        value = product.astype(BF16).astype(F32)
        square = value * value
        high = square.astype(BF16)
        low = (square - high.astype(F32)).astype(BF16)
        total = jnp.dot(high, ones_blocks[...], preferred_element_type=F32)
        total = total + jnp.dot(low, ones_blocks[...], preferred_element_type=F32)
        return (value * lax.rsqrt(total + EPSILON)).astype(BF16)

    def key_value(row):
        source = att[row]
        keys[row] = unit(
            jnp.dot(source, proj_ref[:, channels : 2 * channels], preferred_element_type=F32)
        )
        values[row] = jnp.dot(
            source, proj_ref[:, 2 * channels :], preferred_element_type=F32
        ).astype(BF16)

    att[0:depth, sent:] = jnp.zeros((depth, longitudes + PAD + TAIL - sent, channels), BF16)
    att[rows + depth :, sent:] = jnp.zeros((depth, longitudes + PAD + TAIL - sent, channels), BF16)

    def edge_row(side):
        edge = 0 if side == 0 else rows - 1
        slot = 0 if side == 0 else rows + 1

        @pl.when(has[side])
        def _():
            x_copy(1 - side).wait_recv()
            ext[slot] = ring_pad(rms(xhalo[side].astype(F32), gain1)).astype(BF16)

        @pl.when(jnp.logical_not(has[side]))
        def _():
            ext[slot] = ring_pad(half_turn(rms(x_ref[edge].astype(F32), gain1))).astype(BF16)

    if rows == 2:
        edge_row(1)
    for r in range(1, rows - 1):
        conv_row(r, r == 1)
    if rows > 2:
        edge_row(1)
    conv_row(rows - 1, rows == 2)
    edge_row(0)
    conv_row(0)

    for r in range(rows):
        key_value(r + depth)
    fetch[7].wait()
    fetch[8].wait()

    def halo_rows(side):
        for step in range(depth):

            @pl.when(has[side])
            def _():
                a_copy(1 - side, step).wait_recv()

        for step in range(depth):
            key_value(step if side == 0 else rows + depth + step)

    head_lane = lax.broadcasted_iota(jnp.int32, (QUERY_BLOCK, channels), 1) // HEAD_WIDTH
    sizes = [KEY_WINDOW] * (ROWS_A - 1) + [KEYS - (ROWS_A - 1) * KEY_WINDOW]

    def attend(r, starts):
        def windows(ref, at):
            return jnp.concatenate(
                [ref[r + a, pl.ds(at, sizes[a])] for a in range(ROWS_A)], axis=0
            )

        seen = bias[r]
        all_scores = []
        for at in starts:
            probe = queries[r, pl.ds(at, QUERY_BLOCK)]
            spread = jnp.concatenate([probe] * HEAD_COUNT, axis=0) * heads[...]
            all_scores.append(
                lax.dot_general(
                    spread,
                    windows(keys, at),
                    (((1,), (1,)), ((), ())),
                    preferred_element_type=F32,
                )
            )
        all_mixed, all_sums = [], []
        for at, scores in zip(starts, all_scores):
            parts, sums = [], []
            for h in range(HEAD_COUNT):
                part = scores[h * QUERY_BLOCK : (h + 1) * QUERY_BLOCK] + seen
                peak = jnp.max(part, axis=-1, keepdims=True)
                part = jnp.exp2((part - peak) * (scale_ref[h] * LOG2E))
                sums.append(jnp.sum(part, axis=-1, keepdims=True))
                parts.append(part.astype(BF16))
            all_mixed.append(
                jnp.dot(
                    jnp.concatenate(parts, axis=0),
                    windows(values, at),
                    preferred_element_type=F32,
                )
            )
            all_sums.append(sums)
        for at, mixed, sums in zip(starts, all_mixed, all_sums):
            result = jnp.zeros((QUERY_BLOCK, channels), F32)
            for h in range(HEAD_COUNT):
                share = mixed[h * QUERY_BLOCK : (h + 1) * QUERY_BLOCK] * (1.0 / sums[h])
                result = jnp.where(head_lane == h, share, result)
            mixture[pl.ds(at, QUERY_BLOCK)] = result.astype(BF16)

    group = GROUP
    while longitudes % (group * QUERY_BLOCK):
        group -= 1

    def attend_row(r):
        def attend_group(b, carry):
            at = pl.multiple_of(b * (group * QUERY_BLOCK), QUERY_BLOCK)
            attend(r, [at + g * QUERY_BLOCK for g in range(group)])
            return carry

        lax.fori_loop(0, longitudes // (group * QUERY_BLOCK), attend_group, 0)
        out_ref[r] = (
            hidden[r] + jnp.dot(mixture[...], final_ref[...], preferred_element_type=F32)
        ).astype(BF16)

    halo_rows(0)
    early = max(rows - depth, 0)
    for r in range(early):
        attend_row(r)
    halo_rows(1)
    for r in range(early, rows):
        attend_row(r)

    for side in range(2):

        @pl.when(has[side])
        def _():
            x_copy(side).wait_send()
            for step in range(depth):
                a_copy(side, step).wait_send()


def on_device(
    grid_inputs,
    stencil_prenorm_scale,
    patch_kernel_profiles,
    channel_mixer_tensor,
    softmax_prenorm_scale,
    probe_lookup_content_projector,
    head_logit_scales,
    final_projector,
    azimuth_reaches,
    *,
    n,
):
    rows, longitudes, channels = grid_inputs.shape
    padded = longitudes + PAD + TAIL
    wide = rows + 2 * PATCH_LAT_EXTENT
    vmem = pl.BlockSpec(memory_space=pltpu.VMEM)
    hbm = pl.BlockSpec(memory_space=pltpu.HBM)
    return pl.pallas_call(
        functools.partial(kernel, n),
        out_shape=jax.ShapeDtypeStruct(grid_inputs.shape, BF16),
        in_specs=[hbm] * 9,
        out_specs=vmem,
        scratch_shapes=[
            pltpu.VMEM(grid_inputs.shape, BF16),
            pltpu.VMEM((1, channels), F32),
            pltpu.VMEM((patch_kernel_profiles.shape[1], rows, 3 * TAPS), F32),
            pltpu.VMEM(channel_mixer_tensor.shape, BF16),
            pltpu.VMEM((1, channels), F32),
            pltpu.VMEM(probe_lookup_content_projector.shape, BF16),
            pltpu.SMEM(head_logit_scales.shape, F32),
            pltpu.VMEM(final_projector.shape, BF16),
            pltpu.SMEM(azimuth_reaches.shape, jnp.int32),
            pltpu.VMEM((2, longitudes, channels), BF16),
            pltpu.VMEM((rows + 2, padded, channels), BF16),
            pltpu.VMEM((16, KEYS), F32),
            pltpu.VMEM((BASIS_COUNT * CONV_BLOCK, KEYS), BF16),
            pltpu.VMEM((longitudes, BASIS_COUNT * channels), BF16),
            pltpu.VMEM((rows, longitudes, channels), F32),
            pltpu.VMEM((wide, padded, channels), BF16),
            pltpu.VMEM((rows, longitudes, channels), BF16),
            pltpu.VMEM((wide, padded, channels), BF16),
            pltpu.VMEM((wide, padded, channels), BF16),
            pltpu.VMEM((rows, QUERY_BLOCK, KEYS), F32),
            pltpu.VMEM((HEAD_COUNT * QUERY_BLOCK, channels), BF16),
            pltpu.VMEM((longitudes, channels), BF16),
            pltpu.SemaphoreType.DMA((2,)),
            pltpu.SemaphoreType.DMA((2,)),
            pltpu.SemaphoreType.DMA((2 * PATCH_LAT_EXTENT,)),
            pltpu.SemaphoreType.DMA((2 * PATCH_LAT_EXTENT,)),
            pltpu.SemaphoreType.DMA((9,)),
        ],
        compiler_params=pltpu.CompilerParams(
            collective_id=0, has_side_effects=True, vmem_limit_bytes=64 * 1024 * 1024
        ),
    )(
        grid_inputs,
        stencil_prenorm_scale.reshape(1, channels),
        patch_kernel_profiles.transpose(1, 0, 2),
        channel_mixer_tensor,
        softmax_prenorm_scale.reshape(1, channels),
        probe_lookup_content_projector,
        head_logit_scales,
        final_projector,
        azimuth_reaches,
    )


def solution(mesh):
    placed = (
        P(("members", "band"), None, None),
        P(),
        P("band", None, None),
        P(),
        P(),
        P(),
        P(),
        P(),
        P("band", None),
    )
    return jax.shard_map(
        functools.partial(on_device, n=mesh.shape["band"]),
        mesh=mesh,
        in_specs=placed,
        out_specs=P(("members", "band"), None, None),
        check_vma=False,
    )
```

profile of v0, /device:TPU:25, one launch (start us, length us, event | category | flops | bytes accessed | tf_op | source)
XLA Modules:
  0.0 26.9 jit_solution(11617075500326476748)
XLA Ops:
  0.0 25.0 %shard_map.91 = bf16[3,384,256]{2,1,0:T(8,128)(2,1)} custom-call(bf16[3,384,256]{2,1,0:T(8,128)(2,1)} %x_hbm.1, f32[1,256]{1,0:T(1,128)} %bitcast.4, f32[9,3,27]{2,1,0:T(4,128)} %bitcast.3, bf16[2304,256]{1,0:T(8,128)(2,1)} %mix_hbm.1, f32[1,256]{1,0:T(1,128)} %bitcast.5, bf16[256,768]{1,0:T(8,128)(2,1)} %proj_hbm.1, f32[8]{0:T(128)} %scale_hbm.1, ...), custom_call_target="tpu_custom_call" | custom-call | tf_op jit(solution)/shard_map/pallas_call | solution.py:422
  25.0 1.9 %copy.11 = bf16[3,384,256]{2,1,0:T(8,128)(2,1)} copy(bf16[3,384,256]{2,1,0:T(8,128)(2,1)} %shard_map.91) | data formatting | bytes 1179648
where the time goes:
time: 27.4 us; the launch traced here: 26.9 us
  Pallas kernels  25 us (91%)
  local copies, waits for them, and re-layouts  1.92 us (7%)
    pallas_call x1, Pallas kernels, on_device(): pl.pallas_call(functools.partial(kernel, n), out_shape=jax.ShapeDtypeStru...  25 us
    unnamed x1, local copies, waits for them, and re-layouts  1.92 us

commit v1 on v0

--- a/solution.py
+++ b/solution.py
@@ -86,37 +86,38 @@
     loads,
 ):
     rows, longitudes, channels = x_ref.shape
+    assert rows > PATCH_LAT_EXTENT
     me = lax.axis_index("band")
-    has_up = me > 0
-    has_down = me < n - 1
     depth = PATCH_LAT_EXTENT
     sent = longitudes + 16
+    far = lax.rem(me, 2)
+    near = 1 - far
+
+    def present(side):
+        other = me + 2 * side - 1
+        return jnp.logical_and(other >= 0, other < n)
 
     def x_copy(side):
         return pltpu.make_async_remote_copy(
-            src_ref=x_hbm.at[0 if side == 0 else rows - 1],
+            src_ref=x_hbm.at[side * (rows - 1)],
             dst_ref=xhalo.at[1 - side],
             send_sem=send_x.at[side],
             recv_sem=recv_x.at[1 - side],
-            device_id={"band": me - 1 if side == 0 else me + 1},
+            device_id={"band": me + 2 * side - 1},
             device_id_type=pl.DeviceIdType.MESH,
         )
 
     def a_copy(side, step):
-        source = depth + step if side == 0 else rows + step
-        target = rows + depth + step if side == 0 else step
-        slot = side * depth + step
-        other = (1 - side) * depth + step
+        source = (1 - side) * depth + side * rows + step
+        target = (1 - side) * (rows + depth) + step
         return pltpu.make_async_remote_copy(
             src_ref=att.at[source, pl.ds(0, sent)],
             dst_ref=att.at[target, pl.ds(0, sent)],
-            send_sem=send_a.at[slot],
-            recv_sem=recv_a.at[other],
-            device_id={"band": me - 1 if side == 0 else me + 1},
+            send_sem=send_a.at[side * depth + step],
+            recv_sem=recv_a.at[(1 - side) * depth + step],
+            device_id={"band": me + 2 * side - 1},
             device_id_type=pl.DeviceIdType.MESH,
         )
-
-    has = (has_up, has_down)
 
     pairs = (
         (x_hbm, x_ref),
@@ -139,7 +140,7 @@
     barrier = pltpu.get_barrier_semaphore()
     for side in range(2):
 
-        @pl.when(has[side])
+        @pl.when(present(side))
         def _():
             pl.semaphore_signal(
                 barrier,
@@ -152,7 +153,7 @@
 
     for side in range(2):
 
-        @pl.when(has[side])
+        @pl.when(present(side))
         def _():
             x_copy(side).start()
 
@@ -203,7 +204,7 @@
 
     fetch[3].wait()
 
-    def conv_row(r, first=False):
+    def conv_row(r, first=False, edge=None):
         build_filters(r)
 
         def conv_block(b, carry):
@@ -240,29 +241,22 @@
             )
         )
 
-        if r < depth:
-
-            @pl.when(has_up)
+        def share(side, step, pole_slot):
+            @pl.when(present(side))
             def _():
-                a_copy(0, r).start()
-
-            if r == 0 or r == 1:
-
-                @pl.when(jnp.logical_not(has_up))
-                def _():
-                    att[depth - 1 - r] = ring_pad(half_turn(normed)).astype(BF16)
-
-        if r >= rows - depth:
-
-            @pl.when(has_down)
+                a_copy(side, step).start()
+
+            @pl.when(jnp.logical_not(present(side)))
             def _():
-                a_copy(1, r - (rows - depth)).start()
-
-            @pl.when(jnp.logical_not(has_down))
-            def _():
-                att[2 * rows + 2 * depth - 1 - (r + depth) + 0] = ring_pad(
-                    half_turn(normed)
-                ).astype(BF16)
+                att[pole_slot] = ring_pad(half_turn(normed)).astype(BF16)
+
+        if edge is not None:
+            share(edge, edge * (depth - 1), (1 - edge) * (depth - 1) + edge * (rows + depth))
+        else:
+            if r < depth:
+                share(0, r, depth - 1 - r)
+            if r >= rows - depth:
+                share(1, r - (rows - depth), 2 * rows + depth - 1 - r)
 
     def unit(product):
         value = product.astype(BF16).astype(F32)
@@ -286,27 +280,24 @@
     att[rows + depth :, sent:] = jnp.zeros((depth, longitudes + PAD + TAIL - sent, channels), BF16)
 
     def edge_row(side):
-        edge = 0 if side == 0 else rows - 1
-        slot = 0 if side == 0 else rows + 1
-
-        @pl.when(has[side])
+        row = side * (rows - 1)
+        slot = side * (rows + 1)
+
+        @pl.when(present(side))
         def _():
             x_copy(1 - side).wait_recv()
             ext[slot] = ring_pad(rms(xhalo[side].astype(F32), gain1)).astype(BF16)
 
-        @pl.when(jnp.logical_not(has[side]))
+        @pl.when(jnp.logical_not(present(side)))
         def _():
-            ext[slot] = ring_pad(half_turn(rms(x_ref[edge].astype(F32), gain1))).astype(BF16)
-
-    if rows == 2:
-        edge_row(1)
+            ext[slot] = ring_pad(half_turn(rms(x_ref[row].astype(F32), gain1))).astype(BF16)
+
+        conv_row(row, edge=side)
+
     for r in range(1, rows - 1):
         conv_row(r, r == 1)
-    if rows > 2:
-        edge_row(1)
-    conv_row(rows - 1, rows == 2)
-    edge_row(0)
-    conv_row(0)
+    edge_row(far)
+    edge_row(near)
 
     for r in range(rows):
         key_value(r + depth)
@@ -316,12 +307,12 @@
     def halo_rows(side):
         for step in range(depth):
 
-            @pl.when(has[side])
+            @pl.when(present(side))
             def _():
                 a_copy(1 - side, step).wait_recv()
 
         for step in range(depth):
-            key_value(step if side == 0 else rows + depth + step)
+            key_value(side * (rows + depth) + step)
 
     head_lane = lax.broadcasted_iota(jnp.int32, (QUERY_BLOCK, channels), 1) // HEAD_WIDTH
     sizes = [KEY_WINDOW] * (ROWS_A - 1) + [KEYS - (ROWS_A - 1) * KEY_WINDOW]
@@ -384,17 +375,16 @@
             hidden[r] + jnp.dot(mixture[...], final_ref[...], preferred_element_type=F32)
         ).astype(BF16)
 
-    halo_rows(0)
-    early = max(rows - depth, 0)
-    for r in range(early):
+    halo_rows(near)
+    attend_row(near * (rows - 1))
+    halo_rows(far)
+    for r in range(1, rows - 1):
         attend_row(r)
-    halo_rows(1)
-    for r in range(early, rows):
-        attend_row(r)
+    attend_row(far * (rows - 1))
 
     for side in range(2):
 
-        @pl.when(has[side])
+        @pl.when(present(side))
         def _():
             x_copy(side).wait_send()
             for step in range(depth):
@@ -421,7 +411,7 @@
     hbm = pl.BlockSpec(memory_space=pltpu.HBM)
     return pl.pallas_call(
         functools.partial(kernel, n),
-        out_shape=jax.ShapeDtypeStruct(grid_inputs.shape, BF16),
+        out_shape=pltpu.VMEM(grid_inputs.shape, BF16),
         in_specs=[hbm] * 9,
         out_specs=vmem,
         scratch_shapes=[
@@ -454,7 +444,7 @@
             pltpu.SemaphoreType.DMA((9,)),
         ],
         compiler_params=pltpu.CompilerParams(
-            collective_id=0, has_side_effects=True, vmem_limit_bytes=64 * 1024 * 1024
+            collective_id=0, has_side_effects=True, vmem_limit_bytes=62 * 1024 * 1024
         ),
     )(
         grid_inputs,

time: 27.4 us -> 25.5 us (0.931)
  local copies, waits for them, and re-layouts: 1.92 us -> 0.82 us
  Pallas kernels: 25 us -> 24.2 us
    unnamed x1, local copies, waits for them, and re-layouts: 1.92 us -> 0.82 us
    pallas_call x1, Pallas kernels: 25 us -> 24.2 us  [on_device(): pl.pallas_call(functools.partial(kernel, n), out_shape=pltpu.VMEM(grid_in...]
where the time goes in v1:
time: 25.5 us; the launch traced here: 25 us
  Pallas kernels  24.2 us (95%)
  local copies, waits for them, and re-layouts  0.82 us (3%)
    pallas_call x1, Pallas kernels, on_device(): pl.pallas_call(functools.partial(kernel, n), out_shape=pltpu.VMEM(grid_in...  24.2 us
    unnamed x1, local copies, waits for them, and re-layouts  0.82 us

profile of v1, /device:TPU:25, one launch (start us, length us, event | category | flops | bytes accessed | tf_op | source)
XLA Modules:
  0.0 25.0 jit_solution(15940492196158883547)
XLA Ops:
  0.0 24.2 %shard_map.91 = bf16[3,384,256]{2,1,0:T(8,128)(2,1)S(1)} custom-call(bf16[3,384,256]{2,1,0:T(8,128)(2,1)} %x_hbm.1, f32[1,256]{1,0:T(1,128)} %bitcast.4, f32[9,3,27]{2,1,0:T(4,128)} %bitcast.3, bf16[2304,256]{1,0:T(8,128)(2,1)} %mix_hbm.1, f32[1,256]{1,0:T(1,128)} %bitcast.5, bf16[256,768]{1,0:T(8,128)(2,1)} %proj_hbm.1, f32[8]{0:T(128)} %scale_hbm.1, ...), custom_call_target="tpu_custom_call" | custom-call | tf_op jit(solution)/shard_map/pallas_call | solution.py:412
  24.2 0.8 %copy.11 = bf16[3,384,256]{2,1,0:T(8,128)(2,1)} copy(bf16[3,384,256]{2,1,0:T(8,128)(2,1)S(1)} %shard_map.91) | data formatting | bytes 1179648

commit v2 on v1

--- a/solution.py
+++ b/solution.py
@@ -22,7 +22,7 @@
 QUERY_BLOCK = 32
 KEY_WINDOW = QUERY_BLOCK + 2 * DISC_REACH
 KEYS = 256
-GROUP = 4
+GROUP = 6
 ROWS_A = 2 * PATCH_LAT_EXTENT + 1
 PAD = DISC_REACH
 TAIL = 24
@@ -89,7 +89,7 @@
     assert rows > PATCH_LAT_EXTENT
     me = lax.axis_index("band")
     depth = PATCH_LAT_EXTENT
-    sent = longitudes + 16
+    sent = longitudes
     far = lax.rem(me, 2)
     near = 1 - far
 
@@ -276,9 +276,6 @@
             source, proj_ref[:, 2 * channels :], preferred_element_type=F32
         ).astype(BF16)
 
-    att[0:depth, sent:] = jnp.zeros((depth, longitudes + PAD + TAIL - sent, channels), BF16)
-    att[rows + depth :, sent:] = jnp.zeros((depth, longitudes + PAD + TAIL - sent, channels), BF16)
-
     def edge_row(side):
         row = side * (rows - 1)
         slot = side * (rows + 1)
@@ -304,15 +301,18 @@
     fetch[7].wait()
     fetch[8].wait()
 
+    def halo_row(side, step):
+        @pl.when(present(side))
+        def _():
+            a_copy(1 - side, step).wait_recv()
+
+        row = side * (rows + depth) + step
+        att[row, longitudes:] = att[row, 0 : PAD + TAIL]
+        key_value(row)
+
     def halo_rows(side):
-        for step in range(depth):
-
-            @pl.when(present(side))
-            def _():
-                a_copy(1 - side, step).wait_recv()
-
-        for step in range(depth):
-            key_value(side * (rows + depth) + step)
+        for inner in range(depth):
+            halo_row(side, side * (depth - 1 - 2 * inner) + inner)
 
     head_lane = lax.broadcasted_iota(jnp.int32, (QUERY_BLOCK, channels), 1) // HEAD_WIDTH
     sizes = [KEY_WINDOW] * (ROWS_A - 1) + [KEYS - (ROWS_A - 1) * KEY_WINDOW]

time: 25.5 us -> 24.9 us (0.976); the launches traced: 25 us -> 24.7 us
  Pallas kernels: 24.2 us -> 23.9 us
    pallas_call x1, Pallas kernels: 24.2 us -> 23.9 us  [on_device(): pl.pallas_call(functools.partial(kernel, n), out_shape=pltpu.VMEM(grid_in...]
where the time goes in v2:
time: 24.9 us; the launch traced here: 24.7 us
  Pallas kernels  23.9 us (96%)
  local copies, waits for them, and re-layouts  0.82 us (3%)
    pallas_call x1, Pallas kernels, on_device(): pl.pallas_call(functools.partial(kernel, n), out_shape=pltpu.VMEM(grid_in...  23.9 us
    unnamed x1, local copies, waits for them, and re-layouts  0.82 us

profile of v2, /device:TPU:25, one launch (start us, length us, event | category | flops | bytes accessed | tf_op | source)
XLA Modules:
  0.0 24.7 jit_solution(14140117407574776903)
XLA Ops:
  0.0 23.9 %shard_map.91 = bf16[3,384,256]{2,1,0:T(8,128)(2,1)S(1)} custom-call(bf16[3,384,256]{2,1,0:T(8,128)(2,1)} %x_hbm.1, f32[1,256]{1,0:T(1,128)} %bitcast.4, f32[9,3,27]{2,1,0:T(4,128)} %bitcast.3, bf16[2304,256]{1,0:T(8,128)(2,1)} %mix_hbm.1, f32[1,256]{1,0:T(1,128)} %bitcast.5, bf16[256,768]{1,0:T(8,128)(2,1)} %proj_hbm.1, f32[8]{0:T(128)} %scale_hbm.1, ...), custom_call_target="tpu_custom_call" | custom-call | tf_op jit(solution)/shard_map/pallas_call | solution.py:412
  23.9 0.8 %copy.11 = bf16[3,384,256]{2,1,0:T(8,128)(2,1)} copy(bf16[3,384,256]{2,1,0:T(8,128)(2,1)S(1)} %shard_map.91) | data formatting | bytes 1179648

commit v3 on v2

--- a/solution.py
+++ b/solution.py
@@ -205,7 +205,8 @@
     fetch[3].wait()
 
     def conv_row(r, first=False, edge=None):
-        build_filters(r)
+        if edge is None:
+            build_filters(r)
 
         def conv_block(b, carry):
             at = pl.multiple_of(b * CONV_BLOCK, CONV_BLOCK)
@@ -279,6 +280,7 @@
     def edge_row(side):
         row = side * (rows - 1)
         slot = side * (rows + 1)
+        build_filters(row)
 
         @pl.when(present(side))
         def _():
@@ -293,11 +295,12 @@
 
     for r in range(1, rows - 1):
         conv_row(r, r == 1)
+        key_value(r + depth)
     edge_row(far)
     edge_row(near)
 
-    for r in range(rows):
-        key_value(r + depth)
+    key_value(depth)
+    key_value(rows - 1 + depth)
     fetch[7].wait()
     fetch[8].wait()
 

time: 24.9 us -> 24.4 us (0.980)
  Pallas kernels: 23.9 us -> 23.4 us
    pallas_call x1, Pallas kernels: 23.9 us -> 23.4 us  [on_device(): pl.pallas_call(functools.partial(kernel, n), out_shape=pltpu.VMEM(grid_in...]
where the time goes in v3:
time: 24.4 us; the launch traced here: 24.3 us
  Pallas kernels  23.4 us (96%)
  local copies, waits for them, and re-layouts  0.82 us (3%)
    pallas_call x1, Pallas kernels, on_device(): pl.pallas_call(functools.partial(kernel, n), out_shape=pltpu.VMEM(grid_in...  23.4 us
    unnamed x1, local copies, waits for them, and re-layouts  0.82 us

profile of v3, /device:TPU:25, one launch (start us, length us, event | category | flops | bytes accessed | tf_op | source)
XLA Modules:
  0.0 24.3 jit_solution(10648948442254224265)
XLA Ops:
  0.0 23.4 %shard_map.91 = bf16[3,384,256]{2,1,0:T(8,128)(2,1)S(1)} custom-call(bf16[3,384,256]{2,1,0:T(8,128)(2,1)} %x_hbm.1, f32[1,256]{1,0:T(1,128)} %bitcast.4, f32[9,3,27]{2,1,0:T(4,128)} %bitcast.3, bf16[2304,256]{1,0:T(8,128)(2,1)} %mix_hbm.1, f32[1,256]{1,0:T(1,128)} %bitcast.5, bf16[256,768]{1,0:T(8,128)(2,1)} %proj_hbm.1, f32[8]{0:T(128)} %scale_hbm.1, ...), custom_call_target="tpu_custom_call" | custom-call | tf_op jit(solution)/shard_map/pallas_call | solution.py:415
  23.5 0.8 %copy.11 = bf16[3,384,256]{2,1,0:T(8,128)(2,1)} copy(bf16[3,384,256]{2,1,0:T(8,128)(2,1)S(1)} %shard_map.91) | data formatting | bytes 1179648
